TPU v7x, 128 devices: a whole 4x4x4 slice. The times are simulated.
128 devices in a mesh: dp: 8 (over y_lo, x), tensor: 16 (over y_hi, z, core).
Axes of the slice: x: 4, y: 4 (y_hi: 2, y_lo: 2; y = y_hi * 2 + y_lo), z: 4, core: 2. Of those that a mesh axis runs over, the one named last changes fastest.
Arguments:
- gradient: bfloat16 [8, 4096, 14336], P('dp', None, 'tensor'), may hold values from -45 to 45
- error_in: bfloat16 [8, 4096, 14336], P('dp', None, 'tensor'), may hold values from -3 to 3
- warm_start: float32 [64, 14336], P(None, 'tensor'), may hold values from -6 to 6
Outputs:
- right_factor: float32 [64, 14336], P(None, 'tensor')
- error_out: bfloat16 [8, 4096, 14336], P('dp', None, 'tensor')
All inputs are finite; a program needn't handle non-finite values.
Results may differ from a plain program's by a relative error of at most 0.001.
Values sent between devices are 32-bit elements; how exact they have to be, the bound alone decides.
A program may use at most 128 MiB of HBM per device.

v0:
```python
import jax
import jax.numpy as jnp
from jax import lax
from jax.sharding import PartitionSpec as P

ITERS = 4


def orthonormal(left):
    for sweep in range(2):
        gram_matrix = jnp.dot(left, left.T, precision=lax.Precision.HIGHEST)
        factor = jnp.linalg.cholesky(gram_matrix)
        left = lax.linalg.triangular_solve(factor, left, left_side=True, lower=True)
    return left


def shards(gradient, error_in, warm_start):
    merged = gradient[0].astype(jnp.float32) + error_in[0].astype(jnp.float32)
    replicas = lax.axis_size("dp")
    right = warm_start
    basis = None
    for sweep in range(ITERS):
        partial_value = lax.dot_general(
            right,
            merged,
            (((1,), (1,)), ((), ())),
            precision=lax.Precision.HIGHEST,
            preferred_element_type=jnp.float32,
        )
        basis = orthonormal(lax.psum(partial_value, ("dp", "tensor")))
        local_right = jnp.dot(basis, merged, precision=lax.Precision.HIGHEST)
        right = lax.psum(local_right, "dp") / replicas
    approx = jnp.dot(basis.T, right, precision=lax.Precision.HIGHEST)
    return (right, (merged - approx).astype(jnp.bfloat16)[None])


def solution(mesh):
    in_specs = (P("dp", None, "tensor"), P("dp", None, "tensor"), P(None, "tensor"))
    out_specs = (P(None, "tensor"), P("dp", None, "tensor"))
    return jax.shard_map(shards, mesh=mesh, in_specs=in_specs, out_specs=out_specs, check_vma=False)
```

profile of v0, /device:TPU:1, one launch (start us, length us, event | category | flops | bytes accessed | tf_op | source)
XLA Modules:
  0.0 1162.9 jit_solution(13998122041207047440)
XLA Ops:
  8.1 21.6 %fusion.18 = f32[64,4096]{1,0:T(8,128)} fusion(f32[64,896]{1,0:T(8,128)S(1)} %copy-done, bf16[1,4096,896]{2,1,0:T(8,128)(2,1)} %param.7, bf16[1,4096,896]{2,1,0:T(8,128)(2,1)} %param.6), kind=kOutput, calls=%fused_computation.20 | convolution fusion | flops 2829582336 | bytes 15958016 | tf_op jit(solution)/shard_map/dot_general | solution.py:23
  30.0 150.5 %all-reduce.9.cloned.1.call-done = f32[64,4096]{1,0:T(8,128)} async-done(((f32[64,4096]{1,0:T(8,128)}), f32[64,4096]{1,0:T(8,128)}) %all-reduce.9.cloned.1.call-update) | async-done | bytes 1048592 | tf_op jit(solution)/shard_map/psum | solution.py:30
  183.1 5.8 cholesky.134
  190.3 4.9 custom-call.12
  198.5 5.8 cholesky.145
  205.7 4.9 custom-call.13
  211.7 13.5 %fusion.12 = f32[64,896]{1,0:T(8,128)} fusion(f32[64,4096]{1,0:T(8,128)S(1)} %fusion.53, bf16[1,4096,896]{2,1,0:T(8,128)(2,1)} %param.7, bf16[1,4096,896]{2,1,0:T(8,128)(2,1)} %param.6), kind=kOutput, calls=%fused_computation.13 | convolution fusion | flops 2829582336 | bytes 15958016 | tf_op jit(solution)/shard_map/dot_general | solution.py:31
  225.7 65.2 %all-reduce.11.cloned.1.call-done = f32[64,896]{1,0:T(8,128)} async-done(((f32[64,896]{1,0:T(8,128)}), f32[64,896]{1,0:T(8,128)}) %all-reduce.11.cloned.1.call-update) | async-done | bytes 229392 | tf_op jit(solution)/shard_map/psum | solution.py:32
  290.9 18.5 %fusion.10 = f32[64,4096]{1,0:T(8,128)} fusion(bf16[1,4096,896]{2,1,0:T(8,128)(2,1)} %param.7, bf16[1,4096,896]{2,1,0:T(8,128)(2,1)} %param.6, f32[64,896]{1,0:T(8,128)} %all-reduce.11.cloned.1.call-done), kind=kOutput, calls=%fused_computation.11 | convolution fusion | flops 2829639680 | bytes 15958016 | tf_op jit(solution)/shard_map/dot_general | solution.py:23
  309.4 153.4 %all-reduce.13.cloned.1.call-done = f32[64,4096]{1,0:T(8,128)} async-done(((f32[64,4096]{1,0:T(8,128)}), f32[64,4096]{1,0:T(8,128)}) %all-reduce.13.cloned.1.call-update) | async-done | bytes 1048592 | tf_op jit(solution)/shard_map/psum | solution.py:30
  465.4 5.8 cholesky.156
  472.6 4.9 custom-call.14
  480.9 5.8 cholesky.167
  488.1 4.9 custom-call.15
  494.0 13.5 %fusion.8 = f32[64,896]{1,0:T(8,128)} fusion(f32[64,4096]{1,0:T(8,128)S(1)} %fusion.47, bf16[1,4096,896]{2,1,0:T(8,128)(2,1)} %param.7, bf16[1,4096,896]{2,1,0:T(8,128)(2,1)} %param.6), kind=kOutput, calls=%fused_computation.9 | convolution fusion | flops 2829582336 | bytes 15958016 | tf_op jit(solution)/shard_map/dot_general | solution.py:31
  507.8 65.4 %all-reduce.15.cloned.1.call-done = f32[64,896]{1,0:T(8,128)} async-done(((f32[64,896]{1,0:T(8,128)}), f32[64,896]{1,0:T(8,128)}) %all-reduce.15.cloned.1.call-update) | async-done | bytes 229392 | tf_op jit(solution)/shard_map/psum | solution.py:32
  573.2 18.5 %fusion.6 = f32[64,4096]{1,0:T(8,128)} fusion(bf16[1,4096,896]{2,1,0:T(8,128)(2,1)} %param.7, bf16[1,4096,896]{2,1,0:T(8,128)(2,1)} %param.6, f32[64,896]{1,0:T(8,128)} %all-reduce.15.cloned.1.call-done), kind=kOutput, calls=%fused_computation.7 | convolution fusion | flops 2829639680 | bytes 15958016 | tf_op jit(solution)/shard_map/dot_general | solution.py:23
  591.8 153.4 %all-reduce.17.cloned.1.call-done = f32[64,4096]{1,0:T(8,128)} async-done(((f32[64,4096]{1,0:T(8,128)}), f32[64,4096]{1,0:T(8,128)}) %all-reduce.17.cloned.1.call-update) | async-done | bytes 1048592 | tf_op jit(solution)/shard_map/psum | solution.py:30
  747.8 5.8 cholesky.178
  755.0 4.9 custom-call.16
  763.2 5.8 cholesky.189
  770.4 4.9 custom-call.17
  776.3 13.5 %fusion.4 = f32[64,896]{1,0:T(8,128)} fusion(f32[64,4096]{1,0:T(8,128)S(1)} %fusion.41, bf16[1,4096,896]{2,1,0:T(8,128)(2,1)} %param.7, bf16[1,4096,896]{2,1,0:T(8,128)(2,1)} %param.6), kind=kOutput, calls=%fused_computation.5 | convolution fusion | flops 2829582336 | bytes 15958016 | tf_op jit(solution)/shard_map/dot_general | solution.py:31
  790.4 65.2 %all-reduce.19.cloned.1.call-done = f32[64,896]{1,0:T(8,128)} async-done(((f32[64,896]{1,0:T(8,128)}), f32[64,896]{1,0:T(8,128)}) %all-reduce.19.cloned.1.call-update) | async-done | bytes 229392 | tf_op jit(solution)/shard_map/psum | solution.py:32
  855.5 18.5 %fusion.2 = f32[64,4096]{1,0:T(8,128)} fusion(bf16[1,4096,896]{2,1,0:T(8,128)(2,1)} %param.7, bf16[1,4096,896]{2,1,0:T(8,128)(2,1)} %param.6, f32[64,896]{1,0:T(8,128)} %all-reduce.19.cloned.1.call-done), kind=kOutput, calls=%fused_computation.3 | convolution fusion | flops 2829639680 | bytes 15958016 | tf_op jit(solution)/shard_map/dot_general | solution.py:23
  874.1 153.4 %all-reduce.21.cloned.1.call-done = f32[64,4096]{1,0:T(8,128)} async-done(((f32[64,4096]{1,0:T(8,128)}), f32[64,4096]{1,0:T(8,128)}) %all-reduce.21.cloned.1.call-update) | async-done | bytes 1048592 | tf_op jit(solution)/shard_map/psum | solution.py:30
  1030.1 5.8 cholesky.200
  1045.5 5.8 cholesky.211
  1052.7 4.9 custom-call.19
  1058.7 13.7 %fusion = f32[64,896]{1,0:T(8,128)} fusion(f32[64,4096]{1,0:T(8,128)S(1)} %fusion.35, bf16[1,4096,896]{2,1,0:T(8,128)(2,1)} %param.7, bf16[1,4096,896]{2,1,0:T(8,128)(2,1)} %param.6), kind=kOutput, calls=%fused_computation.1 | convolution fusion | flops 2829582336 | bytes 15958016 | tf_op jit(solution)/shard_map/dot_general | solution.py:31
  1072.4 65.6 %all-reduce.23.cloned.1.call-done = f32[64,896]{1,0:T(8,128)} async-done(((f32[64,896]{1,0:T(8,128)}), f32[64,896]{1,0:T(8,128)}) %all-reduce.23.cloned.1.call-update) | async-done | bytes 229392 | tf_op jit(solution)/shard_map/psum | solution.py:32
  1138.9 17.0 %fusion.17 = bf16[1,4096,896]{2,1,0:T(8,128)(2,1)} fusion(f32[64,4096]{1,0:T(8,128)S(1)} %fusion.35, f32[64,896]{1,0:T(8,128)S(1)} %broadcast_multiply_fusion, bf16[1,4096,896]{2,1,0:T(8,128)(2,1)} %param.7, bf16[1,4096,896]{2,1,0:T(8,128)(2,1)} %param.6), kind=kOutput, calls=%fused_computation.19 | convolution fusion | flops 2836922368 | bytes 23298048 | tf_op jit(solution)/shard_map/dot_general | solution.py:33
  (78 shorter events, 46.9 us)
Async XLA Ops:
  7.2 0.9 copy-start
  7.2 173.3 %all-reduce.9.cloned.1.call-start = ((), (), s32[]{:S(2)}) async-start(), calls=%async_computation | async-start | bytes 2097152 | tf_op jit(solution)/shard_map/psum | solution.py:30
  29.8 261.1 %all-reduce.11.cloned.1.call-start = ((), (), s32[]{:S(2)}) async-start(), calls=%async_computation.1 | async-start | bytes 458752 | tf_op jit(solution)/shard_map/psum | solution.py:32
  225.3 237.6 %all-reduce.13.cloned.1.call-start = ((), (), s32[]{:S(2)}) async-start(), calls=%async_computation.2 | async-start | bytes 2097152 | tf_op jit(solution)/shard_map/psum | solution.py:30
  309.4 263.8 %all-reduce.15.cloned.1.call-start = ((), (), s32[]{:S(2)}) async-start(), calls=%async_computation.3 | async-start | bytes 458752 | tf_op jit(solution)/shard_map/psum | solution.py:32
  507.6 237.6 %all-reduce.17.cloned.1.call-start = ((), (), s32[]{:S(2)}) async-start(), calls=%async_computation.4 | async-start | bytes 2097152 | tf_op jit(solution)/shard_map/psum | solution.py:30
  591.7 263.8 %all-reduce.19.cloned.1.call-start = ((), (), s32[]{:S(2)}) async-start(), calls=%async_computation.5 | async-start | bytes 458752 | tf_op jit(solution)/shard_map/psum | solution.py:32
  789.9 237.6 %all-reduce.21.cloned.1.call-start = ((), (), s32[]{:S(2)}) async-start(), calls=%async_computation.6 | async-start | bytes 2097152 | tf_op jit(solution)/shard_map/psum | solution.py:30
  874.0 263.9 %all-reduce.23.cloned.1.call-start = ((), (), s32[]{:S(2)}) async-start(), calls=%async_computation.7 | async-start | bytes 458752 | tf_op jit(solution)/shard_map/psum | solution.py:32
  1138.9 17.0 %copy-start.1 = (f32[64,896]{1,0:T(8,128)}, f32[64,896]{1,0:T(8,128)S(1)}, u32[]{:S(2)}) copy-start(f32[64,896]{1,0:T(8,128)S(1)} %broadcast_multiply_fusion) | copy-start | bytes 688132
Sparse Core Ops, SparseCore 0:
  29.9 150.5 all-reduce.8
  225.4 65.4 all-reduce.10
  309.5 153.2 all-reduce.12
  507.7 65.4 all-reduce.14
  591.8 153.2 all-reduce.16
  790.0 65.4 all-reduce.18
  874.2 153.2 all-reduce.20
  1072.5 65.4 all-reduce.22
where the time goes:
time: 1170 us; the launch traced here: 1160 us
  waiting for transfers between devices  872 us (75%)
  matrix products  176 us (15%)
  other arithmetic  97.6 us (8%)
  between operations  14.7 us (1%)
    psum x4, waiting for transfers between devices, shards(): basis = orthonormal(lax.psum(partial_value, ('dp', 'tensor')))  611 us
    psum x4, waiting for transfers between devices, shards(): right = lax.psum(local_right, 'dp') / replicas  261 us
    dot_general x4, matrix products, shards(): lax.dot_general(right, merged, (((1,), (1,)), ((), ())), precision=lax.Pr...  77.1 us
    dot_general x4, matrix products, shards(): local_right = jnp.dot(basis, merged, precision=lax.Precision.HIGHEST)  54.3 us
    another operation x24, other arithmetic, orthonormal(): factor = jnp.linalg.cholesky(gram_matrix)  52.2 us
    another operation x16, other arithmetic, orthonormal(): left = lax.linalg.triangular_solve(factor, left, left_side=True, lower=True)  44.4 us
  transfers between devices with their start and end apart: 8, of which 8 were waited for; matrix products, arithmetic and copies ran while one was open for 0% of the time, Pallas kernels for 0%

commit v1 on v0

v1 whole, which is shorter than its diff:
```python
import jax
import jax.numpy as jnp
from jax import lax
from jax.experimental import pallas as pl
from jax.experimental.pallas import tpu as pltpu
from jax.sharding import PartitionSpec as P

ITERS = 4
REPL = 8
R = 64
D = 4096
COLS = 896
CHUNKS = 4
ROWS = D // CHUNKS
PIECE = 16
BLOCK = 512
MESH = pl.DeviceIdType.MESH
F32 = jnp.float32
BF16 = jnp.bfloat16
HIGHEST = lax.Precision.HIGHEST


def hops(step):
    return min(step, 4 - step)


OFFSETS = sorted(
    [(i, j, k) for i in range(4) for j in range(4) for k in range(4) if i + j + k],
    key=lambda o: -sum(map(hops, o)),
)


def terms(value):
    high = value.astype(BF16)
    rest = value - high.astype(F32)
    middle = rest.astype(BF16)
    low = (rest - middle.astype(F32)).astype(BF16)
    return high, middle, low


def sum_terms(product):
    return product[0:R] + product[R : 2 * R] + product[2 * R : 3 * R]


def contract(a, b, dim_a, dim_b, precision=None):
    return lax.dot_general(
        a, b, (((dim_a,), (dim_b,)), ((), ())), precision=precision, preferred_element_type=F32
    )


def inverse_cholesky(gram):
    ahead = 8
    lane = lax.broadcasted_iota(jnp.int32, (R, 2 * R), 1)
    sub = lax.broadcasted_iota(jnp.int32, (R, 2 * R), 0)
    work = jnp.concatenate([gram, jnp.zeros((R, R), F32)], axis=1)
    work = jnp.where(lane == sub + R, 1.0, work)
    for j in range(0, R, ahead):
        cols = [jnp.broadcast_to(work[:, j + k : j + k + 1], (R, 2 * R)) for k in range(ahead)]
        rows = [work[j + k : j + k + 1, :] for k in range(ahead)]
        factors = []
        for k in range(ahead):
            pivot = 1.0 / cols[k][j + k : j + k + 1, :]
            factor = jnp.where(sub > j + k, cols[k] * pivot, 0.0)
            factors.append(factor)
            for m in range(k + 1, ahead):
                cols[m] = cols[m] - factor * cols[m][j + k : j + k + 1, :]
                rows[m] = rows[m] - factor[j + m : j + m + 1, :] * rows[k]
        for k in range(ahead):
            work = work - factors[k] * rows[k]
    diagonal = jnp.sum(jnp.where(lane == sub, work, 0.0), axis=1, keepdims=True)
    return work[:, R:] * lax.rsqrt(diagonal)


def kernel(
    gradient, error, warm, right_out, error_out,
    both, rr, part, cross, mine, slots, left, flat, raw_part, raw_slots, raw, basis_terms, stage,
    load_sem, cross_send, cross_recv, rs_send, rs_recv, ag_send, ag_recv, fwd_send, fwd_recv,
    dp_send, dp_recv, dpg_send, dpg_recv, out_sem,
):
    d, t = lax.axis_index("dp"), lax.axis_index("tensor")
    x, y, z, c = d % 4, (t // 8) * 2 + d // 4, (t // 2) % 4, t % 2
    other = 1 - c
    group = (x + y + z) % 4
    place = x * 4 + y
    chip = place * 4 + z
    own = group * 32 + c * 16 + place

    def device(i, j, k):
        return ((j % 2) * 4 + i, (j // 2) * 8 + k * 2 + c)

    def away(o):
        return device((x + o[0]) % 4, (y + o[1]) % 4, (z + o[2]) % 4)

    sibling = (d, (t // 2) * 2 + other)

    def load(j):
        rows = pl.ds(j * ROWS, ROWS)
        return (
            pltpu.make_async_copy(gradient.at[0, rows], both.at[rows, 0:COLS], load_sem.at[j, 0]),
            pltpu.make_async_copy(error.at[0, rows], both.at[rows, COLS : 2 * COLS], load_sem.at[j, 1]),
        )

    for j in range(CHUNKS):
        for copy in load(j):
            copy.start()

    barrier = pltpu.get_barrier_semaphore()
    for o in OFFSETS:
        pl.semaphore_signal(barrier, 1, device_id=away(o), device_id_type=MESH)
    pl.semaphore_signal(barrier, 1, device_id=sibling, device_id_type=MESH)

    def set_right(value):
        for i, term in enumerate(terms(value)):
            rr[i * R : (i + 1) * R, 0:COLS] = term
            rr[i * R : (i + 1) * R, COLS : 2 * COLS] = term

    set_right(warm[...])
    pl.semaphore_wait(barrier, len(OFFSETS) + 1)

    def remote(src, dst, send, recv, target):
        return pltpu.make_async_remote_copy(src, dst, send, recv, device_id=target, device_id_type=MESH)

    def cross_copy(j):
        return remote(part.at[pl.ds(j * 32 + other * 16, 16)], cross.at[j], cross_send.at[j], cross_recv.at[j], sibling)

    def fwd_copy(j):
        half = left.at[pl.ds(j * 32 + c * 16, 16)]
        return remote(half, half, fwd_send.at[j], fwd_recv.at[j], sibling)

    def left_chunk(j):
        rows = pl.ds(pl.multiple_of(j * ROWS, ROWS), ROWS)
        product = sum_terms(contract(rr[...], both[rows, :], 1, 1))
        for b in range(8):
            part[pl.ds(j * 32 + b * 4, 4)] = product[:, b * 128 : (b + 1) * 128].reshape(4, PIECE, 128)
        cross_copy(j).start()

    def scatter_chunk(j):
        cross_copy(j).wait_recv()
        mine[j] = part[pl.ds(j * 32 + c * 16, 16)] + cross[j]
        for r in (10, 2, 8, 6, 14, 9, 11, 5, 7, 13, 15, 1, 3, 4, 12, 0):
            i, k = (x + r // 4) % 4, (y + r % 4) % 4
            copy = remote(mine.at[j, i * 4 + k], slots.at[chip], rs_send, rs_recv, device(i, k, (j - i - k + 8) % 4))
            if r:
                copy.start()
            else:

                @pl.when(j != group)
                def _():
                    copy.start()

                @pl.when(j == group)
                def _():
                    slots[chip] = mine[j, place]

    def right_chunk(j, gram):
        @pl.when(j == group)
        def _():
            remote(left.at[0:15], left.at[0:15], ag_send, ag_recv.at[j], sibling).wait_recv()

        @pl.when(j != group)
        def _():
            remote(left.at[0:16], left.at[0:16], ag_send, ag_recv.at[j], sibling).wait_recv()

        fwd_copy(j).start()
        fwd_copy(j).wait_recv()
        rows = pl.ds(pl.multiple_of(j * ROWS, ROWS), ROWS)
        blocks = left[pl.ds(j * 32, 32)].reshape(8, R, 128)
        value = jnp.concatenate([blocks[b] for b in range(8)], axis=1)
        flat[:, rows] = value
        stacked = jnp.concatenate(terms(value), axis=0)
        product = sum_terms(contract(stacked, both[rows, :], 1, 0))
        raw_part[...] += product[:, 0:COLS] + product[:, COLS : 2 * COLS]
        return gram + contract(value, value, 1, 1, HIGHEST)

    def ranks(owner):
        return pl.ds(pl.multiple_of(owner * 8, 8), 8)

    def iteration(step, _):
        def left_step(j, carry):
            @pl.when(step == 0)
            def _():
                rows = pl.ds(pl.multiple_of(j * ROWS, ROWS), ROWS)
                pltpu.make_async_copy(gradient.at[0, rows], both.at[rows, 0:COLS], load_sem.at[j, 0]).wait()
                pltpu.make_async_copy(error.at[0, rows], both.at[rows, COLS : 2 * COLS], load_sem.at[j, 1]).wait()

            left_chunk(j)

            @pl.when(j > 0)
            def _():
                scatter_chunk(j - 1)

            return carry

        lax.fori_loop(0, CHUNKS, left_step, 0)
        scatter_chunk(CHUNKS - 1)
        raw_part[...] = jnp.zeros_like(raw_part)
        remote(slots.at[0:63], slots.at[0:63], rs_send, rs_recv, sibling).wait_recv()
        left[own] = jnp.sum(slots[...], axis=0)
        for o in OFFSETS:
            remote(left.at[own], left.at[own], ag_send, ag_recv.at[group], away(o)).start()

        gram = lax.fori_loop(0, CHUNKS, right_chunk, jnp.zeros((R, R), F32))

        def dp_device(k):
            return lax.rem(d + k, REPL)

        for k in (6, 2, 5, 7, 1, 3, 4):
            owner = dp_device(k)
            remote(raw_part.at[ranks(owner)], raw_slots.at[d], dp_send, dp_recv, (owner, t)).start()
        raw_slots[d] = raw_part[ranks(d)]

        first = inverse_cholesky(gram)
        left_one = jnp.dot(first, flat[...], precision=HIGHEST, preferred_element_type=F32)
        flat[...] = left_one
        gram_two = contract(left_one, left_one, 1, 1, HIGHEST)

        remote(raw_slots.at[0:7], raw_slots.at[0:7], dp_send, dp_recv, sibling).wait_recv()
        raw[ranks(d)] = jnp.sum(raw_slots[...], axis=0)
        for k in (6, 2, 5, 7, 1, 3, 4):
            remote(raw.at[ranks(d)], raw.at[ranks(d)], dpg_send, dpg_recv, (dp_device(k), t)).start()

        second = inverse_cholesky(gram_two)

        @pl.when(step == ITERS - 1)
        def _():
            basis = jnp.dot(second, flat[...], precision=HIGHEST, preferred_element_type=F32)
            high, middle, _ = terms(basis)
            for i, term in enumerate((high, middle, high, middle)):
                basis_terms[i * R : (i + 1) * R] = term

        both_sweeps = jnp.dot(second, first, precision=HIGHEST, preferred_element_type=F32) * (1.0 / REPL)

        for j in range(CHUNKS):
            cross_copy(j).wait_send()
            fwd_copy(j).wait_send()
        remote(slots.at[0:63], slots.at[0:63], rs_send, rs_recv, sibling).wait_send()
        remote(left.at[0:63], left.at[0:63], ag_send, ag_recv.at[0], sibling).wait_send()
        remote(raw_slots.at[0:7], raw_slots.at[0:7], dp_send, dp_recv, sibling).wait_send()
        remote(raw_slots.at[0:7], raw_slots.at[0:7], dpg_send, dpg_recv, sibling).wait()

        right = jnp.dot(both_sweeps, raw[...], precision=HIGHEST, preferred_element_type=F32)
        right_out[...] = right
        set_right(right)
        return 0

    lax.fori_loop(0, ITERS, iteration, 0)

    high, middle, _ = terms(right_out[...])
    right_terms = jnp.concatenate([high, high, middle, middle], axis=0)

    def out_copy(b, slot):
        rows = pl.ds(pl.multiple_of(b * BLOCK, BLOCK), BLOCK)
        return pltpu.make_async_copy(stage.at[slot], error_out.at[0, rows], out_sem.at[slot])

    def finish(b, _):
        slot = lax.rem(b, 2)

        @pl.when(b >= 2)
        def _():
            out_copy(b - 2, slot).wait()

        rows = pl.ds(pl.multiple_of(b * BLOCK, BLOCK), BLOCK)
        approx = contract(basis_terms[:, rows], right_terms, 0, 0)
        block = both[rows, :]
        merged = block[:, 0:COLS].astype(F32) + block[:, COLS : 2 * COLS].astype(F32)
        stage[slot] = (merged - approx).astype(BF16)
        out_copy(b, slot).start()
        return 0

    count = D // BLOCK
    lax.fori_loop(0, count, finish, 0)
    out_copy(count - 2, count % 2).wait()
    out_copy(count - 1, (count - 1) % 2).wait()


def shards(gradient, error_in, warm_start):
    dma = pltpu.SemaphoreType.DMA
    return pl.pallas_call(
        kernel,
        name="power_iterations",
        out_shape=(
            jax.ShapeDtypeStruct((R, COLS), F32),
            jax.ShapeDtypeStruct((1, D, COLS), BF16),
        ),
        in_specs=[
            pl.BlockSpec(memory_space=pl.ANY),
            pl.BlockSpec(memory_space=pl.ANY),
            pl.BlockSpec(memory_space=pltpu.VMEM),
        ],
        out_specs=(pl.BlockSpec(memory_space=pltpu.VMEM), pl.BlockSpec(memory_space=pl.ANY)),
        scratch_shapes=[
            pltpu.VMEM((D, 2 * COLS), BF16),
            pltpu.VMEM((3 * R, 2 * COLS), BF16),
            pltpu.VMEM((128, PIECE, 128), F32),
            pltpu.VMEM((CHUNKS, 16, PIECE, 128), F32),
            pltpu.VMEM((CHUNKS, 16, PIECE, 128), F32),
            pltpu.VMEM((64, PIECE, 128), F32),
            pltpu.VMEM((128, PIECE, 128), F32),
            pltpu.VMEM((R, D), F32),
            pltpu.VMEM((R, COLS), F32),
            pltpu.VMEM((REPL, 8, COLS), F32),
            pltpu.VMEM((R, COLS), F32),
            pltpu.VMEM((4 * R, D), BF16),
            pltpu.VMEM((2, BLOCK, COLS), BF16),
            dma((CHUNKS, 2)),
            dma((CHUNKS,)),
            dma((CHUNKS,)),
            dma(()),
            dma(()),
            dma(()),
            dma((CHUNKS,)),
            dma((CHUNKS,)),
            dma((CHUNKS,)),
            dma(()),
            dma(()),
            dma(()),
            dma(()),
            dma((2,)),
        ],
        compiler_params=pltpu.CompilerParams(
            collective_id=0, has_side_effects=True, vmem_limit_bytes=56 * 1024 * 1024
        ),
    )(gradient, error_in, warm_start)


def solution(mesh):
    in_specs = (P("dp", None, "tensor"), P("dp", None, "tensor"), P(None, "tensor"))
    out_specs = (P(None, "tensor"), P("dp", None, "tensor"))
    return jax.shard_map(shards, mesh=mesh, in_specs=in_specs, out_specs=out_specs, check_vma=False)
```

time: 1170 us -> 195 us (0.17)
  waiting for transfers between devices: 872 us -> 0 us
  Pallas kernels: 0 us -> 186 us
  matrix products: 176 us -> 0 us
  other arithmetic: 97.6 us -> 0 us
  between operations: 14.7 us -> 0.64 us
    psum x8 -> x0, waiting for transfers between devices: 872 us -> none  [the longest x4 611 us: shards(): basis = orthonormal(lax.psum(partial_value, ('dp', 'tensor')))]
    pallas_call x0 -> x1, Pallas kernels: none -> 186 us  [shards(): pl.pallas_call(kernel, name='power_iterations', out_shape=(jax.ShapeDtype...]
    dot_general x17 -> x0, matrix products: 162 us -> none  [the longest x4 77.1 us: shards(): lax.dot_general(right, merged, (((1,), (1,)), ((), ())), precision=lax.Pr...]
    another operation x40 -> x0, other arithmetic: 96.5 us -> none  [the longest x24 52.2 us: orthonormal(): factor = jnp.linalg.cholesky(gram_matrix)]
    another operation x8 -> x0, matrix products: 13.3 us -> none  [orthonormal(): left = lax.linalg.triangular_solve(factor, left, left_side=True, lower=True)]
  transfers between devices with their start and end apart: 8 -> 0, of which waited for: 8 -> 0; matrix products, arithmetic and copies ran while one was open for 0% -> 0% of each run, Pallas kernels for 0% -> 0%
where the time goes in v1:
time: 195 us
  Pallas kernels  186 us (95%)
  local copies, waits for them, and re-layouts  8.36 us (4%)
    pallas_call x1, Pallas kernels, shards(): pl.pallas_call(kernel, name='power_iterations', out_shape=(jax.ShapeDtype...  186 us
    unnamed x2, local copies, waits for them, and re-layouts  8.36 us

profile of v1, /device:TPU:1, one launch (start us, length us, event | category | flops | bytes accessed | tf_op | source)
XLA Modules:
  0.0 195.1 jit_solution(1507039162980451326)
XLA Ops:
  0.6 186.1 %power_iterations.1 = (f32[64,896]{1,0:T(8,128)}, bf16[1,4096,896]{2,1,0:T(8,128)(2,1)}) custom-call(bf16[1,4096,896]{2,1,0:T(8,128)(2,1)} %gradient.1, bf16[1,4096,896]{2,1,0:T(8,128)(2,1)} %error.1, f32[64,896]{1,0:T(8,128)} %warm.1), custom_call_target="tpu_custom_call" | custom-call | tf_op jit(solution)/shard_map/power_iterations/pallas_call | solution.py:278
  186.7 1.6 copy.7
  188.4 6.7 %copy.8 = bf16[1,4096,896]{2,1,0:T(8,128)(2,1)} copy(bf16[1,4096,896]{2,1,0:T(8,128)(2,1)} %get-tuple-element.5) | data formatting | bytes 14680064

commit v2 on v1

--- a/solution.py
+++ b/solution.py
@@ -14,6 +14,7 @@
 ROWS = D // CHUNKS
 PIECE = 16
 BLOCK = 512
+VMEM_LIMIT = 58 * 1024 * 1024
 MESH = pl.DeviceIdType.MESH
 F32 = jnp.float32
 BF16 = jnp.bfloat16
@@ -72,10 +73,10 @@
 
 
 def kernel(
-    gradient, error, warm, right_out, error_out,
-    both, rr, part, cross, mine, slots, left, flat, raw_part, raw_slots, raw, basis_terms, stage,
+    gradient, error, warm, basis_terms, right_out,
+    both, turned, rr, part, cross, mine, slots, left, flat, raw_part, raw_slots, raw, sweeps,
     load_sem, cross_send, cross_recv, rs_send, rs_recv, ag_send, ag_recv, fwd_send, fwd_recv,
-    dp_send, dp_recv, dpg_send, dpg_recv, out_sem,
+    dp_send, dp_recv, dpg_send, dpg_recv,
 ):
     d, t = lax.axis_index("dp"), lax.axis_index("tensor")
     x, y, z, c = d % 4, (t // 8) * 2 + d // 4, (t // 2) % 4, t % 2
@@ -115,7 +116,6 @@
             rr[i * R : (i + 1) * R, COLS : 2 * COLS] = term
 
     set_right(warm[...])
-    pl.semaphore_wait(barrier, len(OFFSETS) + 1)
 
     def remote(src, dst, send, recv, target):
         return pltpu.make_async_remote_copy(src, dst, send, recv, device_id=target, device_id_type=MESH)
@@ -127,12 +127,22 @@
         half = left.at[pl.ds(j * 32 + c * 16, 16)]
         return remote(half, half, fwd_send.at[j], fwd_recv.at[j], sibling)
 
-    def left_chunk(j):
-        rows = pl.ds(pl.multiple_of(j * ROWS, ROWS), ROWS)
-        product = sum_terms(contract(rr[...], both[rows, :], 1, 1))
+    def keep(j, product):
+        product = sum_terms(product)
         for b in range(8):
             part[pl.ds(j * 32 + b * 4, 4)] = product[:, b * 128 : (b + 1) * 128].reshape(4, PIECE, 128)
-        cross_copy(j).start()
+
+    def row_chunk(j):
+        return pl.ds(pl.multiple_of(j * ROWS, ROWS), ROWS)
+
+    def loaded(j):
+        rows = row_chunk(j)
+        pltpu.make_async_copy(gradient.at[0, rows], both.at[rows, 0:COLS], load_sem.at[j, 0]).wait()
+        pltpu.make_async_copy(error.at[0, rows], both.at[rows, COLS : 2 * COLS], load_sem.at[j, 1]).wait()
+
+    def first_product(j):
+        loaded(j)
+        keep(j, contract(rr[...], both[row_chunk(j), :], 1, 1))
 
     def scatter_chunk(j):
         cross_copy(j).wait_recv()
@@ -152,7 +162,7 @@
                 def _():
                     slots[chip] = mine[j, place]
 
-    def right_chunk(j, gram):
+    def gathered(j):
         @pl.when(j == group)
         def _():
             remote(left.at[0:15], left.at[0:15], ag_send, ag_recv.at[j], sibling).wait_recv()
@@ -162,6 +172,12 @@
             remote(left.at[0:16], left.at[0:16], ag_send, ag_recv.at[j], sibling).wait_recv()
 
         fwd_copy(j).start()
+
+    def right_chunk(j, carry):
+        @pl.when(j < CHUNKS - 1)
+        def _():
+            gathered(j + 1)
+
         fwd_copy(j).wait_recv()
         rows = pl.ds(pl.multiple_of(j * ROWS, ROWS), ROWS)
         blocks = left[pl.ds(j * 32, 32)].reshape(8, R, 128)
@@ -170,20 +186,25 @@
         stacked = jnp.concatenate(terms(value), axis=0)
         product = sum_terms(contract(stacked, both[rows, :], 1, 0))
         raw_part[...] += product[:, 0:COLS] + product[:, COLS : 2 * COLS]
-        return gram + contract(value, value, 1, 1, HIGHEST)
+        return carry
 
     def ranks(owner):
         return pl.ds(pl.multiple_of(owner * 8, 8), 8)
 
+    first_product(0)
+    pl.semaphore_wait(barrier, len(OFFSETS) + 1)
+
     def iteration(step, _):
         def left_step(j, carry):
-            @pl.when(step == 0)
+            @pl.when((step == 0) & (j > 0))
             def _():
-                rows = pl.ds(pl.multiple_of(j * ROWS, ROWS), ROWS)
-                pltpu.make_async_copy(gradient.at[0, rows], both.at[rows, 0:COLS], load_sem.at[j, 0]).wait()
-                pltpu.make_async_copy(error.at[0, rows], both.at[rows, COLS : 2 * COLS], load_sem.at[j, 1]).wait()
-
-            left_chunk(j)
+                first_product(j)
+
+            @pl.when(step > 0)
+            def _():
+                keep(j, jnp.dot(rr[...], turned[:, row_chunk(j)], preferred_element_type=F32))
+
+            cross_copy(j).start()
 
             @pl.when(j > 0)
             def _():
@@ -193,13 +214,24 @@
 
         lax.fori_loop(0, CHUNKS, left_step, 0)
         scatter_chunk(CHUNKS - 1)
+
+        @pl.when(step == 0)
+        def _():
+            def turn(j, carry):
+                rows = pl.ds(pl.multiple_of(j * BLOCK, BLOCK), BLOCK)
+                turned[:, rows] = both[rows, :].T
+                return carry
+
+            lax.fori_loop(0, D // BLOCK, turn, 0)
+
         raw_part[...] = jnp.zeros_like(raw_part)
         remote(slots.at[0:63], slots.at[0:63], rs_send, rs_recv, sibling).wait_recv()
         left[own] = jnp.sum(slots[...], axis=0)
         for o in OFFSETS:
             remote(left.at[own], left.at[own], ag_send, ag_recv.at[group], away(o)).start()
 
-        gram = lax.fori_loop(0, CHUNKS, right_chunk, jnp.zeros((R, R), F32))
+        gathered(0)
+        lax.fori_loop(0, CHUNKS, right_chunk, 0)
 
         def dp_device(k):
             return lax.rem(d + k, REPL)
@@ -209,26 +241,29 @@
             remote(raw_part.at[ranks(owner)], raw_slots.at[d], dp_send, dp_recv, (owner, t)).start()
         raw_slots[d] = raw_part[ranks(d)]
 
-        first = inverse_cholesky(gram)
-        left_one = jnp.dot(first, flat[...], precision=HIGHEST, preferred_element_type=F32)
-        flat[...] = left_one
-        gram_two = contract(left_one, left_one, 1, 1, HIGHEST)
+        @pl.when(step < ITERS)
+        def _():
+            sweeps[0] = inverse_cholesky(contract(flat[...], flat[...], 1, 1, HIGHEST))
 
         remote(raw_slots.at[0:7], raw_slots.at[0:7], dp_send, dp_recv, sibling).wait_recv()
         raw[ranks(d)] = jnp.sum(raw_slots[...], axis=0)
         for k in (6, 2, 5, 7, 1, 3, 4):
             remote(raw.at[ranks(d)], raw.at[ranks(d)], dpg_send, dpg_recv, (dp_device(k), t)).start()
 
-        second = inverse_cholesky(gram_two)
+        @pl.when(step < ITERS)
+        def _():
+            first = sweeps[0]
+            left_one = jnp.dot(first, flat[...], precision=HIGHEST, preferred_element_type=F32)
+            flat[...] = left_one
+            second = inverse_cholesky(contract(left_one, left_one, 1, 1, HIGHEST))
+            sweeps[1] = second
+            sweeps[0] = jnp.dot(second, first, precision=HIGHEST, preferred_element_type=F32) * (1.0 / REPL)
 
         @pl.when(step == ITERS - 1)
         def _():
-            basis = jnp.dot(second, flat[...], precision=HIGHEST, preferred_element_type=F32)
+            basis = jnp.dot(sweeps[1], flat[...], precision=HIGHEST, preferred_element_type=F32)
             high, middle, _ = terms(basis)
-            for i, term in enumerate((high, middle, high, middle)):
-                basis_terms[i * R : (i + 1) * R] = term
-
-        both_sweeps = jnp.dot(second, first, precision=HIGHEST, preferred_element_type=F32) * (1.0 / REPL)
+            basis_terms[...] = jnp.concatenate([high, middle, high, middle], axis=0).T
 
         for j in range(CHUNKS):
             cross_copy(j).wait_send()
@@ -238,58 +273,46 @@
         remote(raw_slots.at[0:7], raw_slots.at[0:7], dp_send, dp_recv, sibling).wait_send()
         remote(raw_slots.at[0:7], raw_slots.at[0:7], dpg_send, dpg_recv, sibling).wait()
 
-        right = jnp.dot(both_sweeps, raw[...], precision=HIGHEST, preferred_element_type=F32)
+        right = jnp.dot(sweeps[0], raw[...], precision=HIGHEST, preferred_element_type=F32)
         right_out[...] = right
         set_right(right)
         return 0
 
     lax.fori_loop(0, ITERS, iteration, 0)
 
-    high, middle, _ = terms(right_out[...])
+
+def finish(gradient, error, basis_terms, right, right_out, error_out):
+    @pl.when(pl.program_id(0) == 0)
+    def _():
+        right_out[...] = right[...]
+
+    high, middle, _ = terms(right[...])
     right_terms = jnp.concatenate([high, high, middle, middle], axis=0)
-
-    def out_copy(b, slot):
-        rows = pl.ds(pl.multiple_of(b * BLOCK, BLOCK), BLOCK)
-        return pltpu.make_async_copy(stage.at[slot], error_out.at[0, rows], out_sem.at[slot])
-
-    def finish(b, _):
-        slot = lax.rem(b, 2)
-
-        @pl.when(b >= 2)
-        def _():
-            out_copy(b - 2, slot).wait()
-
-        rows = pl.ds(pl.multiple_of(b * BLOCK, BLOCK), BLOCK)
-        approx = contract(basis_terms[:, rows], right_terms, 0, 0)
-        block = both[rows, :]
-        merged = block[:, 0:COLS].astype(F32) + block[:, COLS : 2 * COLS].astype(F32)
-        stage[slot] = (merged - approx).astype(BF16)
-        out_copy(b, slot).start()
-        return 0
-
-    count = D // BLOCK
-    lax.fori_loop(0, count, finish, 0)
-    out_copy(count - 2, count % 2).wait()
-    out_copy(count - 1, (count - 1) % 2).wait()
+    approx = jnp.dot(basis_terms[...], right_terms, preferred_element_type=F32)
+    merged = gradient[0].astype(F32) + error[0].astype(F32)
+    error_out[0] = (merged - approx).astype(BF16)
 
 
 def shards(gradient, error_in, warm_start):
     dma = pltpu.SemaphoreType.DMA
-    return pl.pallas_call(
+    block = pl.BlockSpec((1, BLOCK, COLS), lambda i: (0, i, 0))
+    whole = pl.BlockSpec(memory_space=pltpu.VMEM)
+    basis_terms, right = pl.pallas_call(
         kernel,
         name="power_iterations",
         out_shape=(
+            jax.ShapeDtypeStruct((D, 4 * R), BF16),
             jax.ShapeDtypeStruct((R, COLS), F32),
-            jax.ShapeDtypeStruct((1, D, COLS), BF16),
         ),
         in_specs=[
-            pl.BlockSpec(memory_space=pl.ANY),
-            pl.BlockSpec(memory_space=pl.ANY),
-            pl.BlockSpec(memory_space=pltpu.VMEM),
+            pl.BlockSpec(memory_space=pltpu.HBM),
+            pl.BlockSpec(memory_space=pltpu.HBM),
+            whole,
         ],
-        out_specs=(pl.BlockSpec(memory_space=pltpu.VMEM), pl.BlockSpec(memory_space=pl.ANY)),
+        out_specs=(whole, whole),
         scratch_shapes=[
             pltpu.VMEM((D, 2 * COLS), BF16),
+            pltpu.VMEM((2 * COLS, D), BF16),
             pltpu.VMEM((3 * R, 2 * COLS), BF16),
             pltpu.VMEM((128, PIECE, 128), F32),
             pltpu.VMEM((CHUNKS, 16, PIECE, 128), F32),
@@ -300,8 +323,7 @@
             pltpu.VMEM((R, COLS), F32),
             pltpu.VMEM((REPL, 8, COLS), F32),
             pltpu.VMEM((R, COLS), F32),
-            pltpu.VMEM((4 * R, D), BF16),
-            pltpu.VMEM((2, BLOCK, COLS), BF16),
+            pltpu.VMEM((2, R, R), F32),
             dma((CHUNKS, 2)),
             dma((CHUNKS,)),
             dma((CHUNKS,)),
@@ -315,12 +337,23 @@
             dma(()),
             dma(()),
             dma(()),
-            dma((2,)),
         ],
         compiler_params=pltpu.CompilerParams(
-            collective_id=0, has_side_effects=True, vmem_limit_bytes=56 * 1024 * 1024
+            collective_id=0, has_side_effects=True, vmem_limit_bytes=VMEM_LIMIT
         ),
     )(gradient, error_in, warm_start)
+    return pl.pallas_call(
+        finish,
+        name="error_feedback",
+        grid=(D // BLOCK,),
+        out_shape=(
+            jax.ShapeDtypeStruct((R, COLS), F32),
+            jax.ShapeDtypeStruct((1, D, COLS), BF16),
+        ),
+        in_specs=[block, block, pl.BlockSpec((BLOCK, 4 * R), lambda i: (i, 0)), whole],
+        out_specs=(whole, block),
+        compiler_params=pltpu.CompilerParams(vmem_limit_bytes=VMEM_LIMIT),
+    )(gradient, error_in, basis_terms, right)
 
 
 def solution(mesh):

time: 195 us -> 168 us (0.86)
  Pallas kernels: 186 us -> 168 us
  local copies, waits for them, and re-layouts: 8.36 us -> 0 us
    pallas_call x1, Pallas kernels: 186 us -> 156 us  [shards(): pl.pallas_call(kernel, name='power_iterations', out_shape=(jax.ShapeDtype...]
    pallas_call x0 -> x1, Pallas kernels: none -> 11.9 us  [shards(): pl.pallas_call(finish, name='error_feedback', grid=(D // BLOCK,), out_sha...]
    unnamed x2 -> x0, local copies, waits for them, and re-layouts: 8.36 us -> none
where the time goes in v2:
time: 168 us
  Pallas kernels  168 us (100%)
    pallas_call x1, Pallas kernels, shards(): pl.pallas_call(kernel, name='power_iterations', out_shape=(jax.ShapeDtype...  156 us
    pallas_call x1, Pallas kernels, shards(): pl.pallas_call(finish, name='error_feedback', grid=(D // BLOCK,), out_sha...  11.9 us

profile of v2, /device:TPU:1, one launch (start us, length us, event | category | flops | bytes accessed | tf_op | source)
XLA Modules:
  0.0 168.2 jit_solution(6815564308687479531)
XLA Ops:
  0.6 155.7 %power_iterations.1 = (bf16[4096,256]{1,0:T(8,128)(2,1)}, f32[64,896]{1,0:T(8,128)}) custom-call(bf16[1,4096,896]{2,1,0:T(8,128)(2,1)} %gradient.3, bf16[1,4096,896]{2,1,0:T(8,128)(2,1)} %error.3, f32[64,896]{1,0:T(8,128)} %warm.1), custom_call_target="tpu_custom_call" | custom-call | tf_op jit(solution)/shard_map/power_iterations/pallas_call | solution.py:300
  156.3 11.9 %error_feedback.1 = (f32[64,896]{1,0:T(8,128)}, bf16[1,4096,896]{2,1,0:T(8,128)(2,1)}) custom-call(bf16[1,4096,896]{2,1,0:T(8,128)(2,1)} %gradient.3, bf16[1,4096,896]{2,1,0:T(8,128)(2,1)} %error.3, bf16[4096,256]{1,0:T(8,128)(2,1)} %get-tuple-element.4.basis_terms, f32[64,896]{1,0:T(8,128)} %get-tuple-element.5.right), custom_call_target="tpu_custom_call" | custom-call | tf_op jit(solution)/shard_map/error_feedback/pallas_call | solution.py:345

commit v3 on v2

--- a/solution.py
+++ b/solution.py
@@ -14,7 +14,7 @@
 ROWS = D // CHUNKS
 PIECE = 16
 BLOCK = 512
-VMEM_LIMIT = 58 * 1024 * 1024
+VMEM_LIMIT = 46 * 1024 * 1024
 MESH = pl.DeviceIdType.MESH
 F32 = jnp.float32
 BF16 = jnp.bfloat16
@@ -29,6 +29,8 @@
     [(i, j, k) for i in range(4) for j in range(4) for k in range(4) if i + j + k],
     key=lambda o: -sum(map(hops, o)),
 )
+
+DP_OFFSETS = ((1, 2), (1, 1), (1, 3), (0, 2), (0, 1), (0, 3), (1, 0))
 
 
 def terms(value):
@@ -188,6 +190,9 @@
         raw_part[...] += product[:, 0:COLS] + product[:, COLS : 2 * COLS]
         return carry
 
+    def dp_device(o):
+        return ((d // 4 + o[0]) % 2) * 4 + (x + o[1]) % 4
+
     def ranks(owner):
         return pl.ds(pl.multiple_of(owner * 8, 8), 8)
 
@@ -206,13 +211,12 @@
 
             cross_copy(j).start()
 
-            @pl.when(j > 0)
-            def _():
-                scatter_chunk(j - 1)
-
             return carry
 
         lax.fori_loop(0, CHUNKS, left_step, 0)
+        scatter_chunk(CHUNKS - 4)
+        scatter_chunk(CHUNKS - 3)
+        scatter_chunk(CHUNKS - 2)
         scatter_chunk(CHUNKS - 1)
 
         @pl.when(step == 0)
@@ -233,10 +237,7 @@
         gathered(0)
         lax.fori_loop(0, CHUNKS, right_chunk, 0)
 
-        def dp_device(k):
-            return lax.rem(d + k, REPL)
-
-        for k in (6, 2, 5, 7, 1, 3, 4):
+        for k in DP_OFFSETS:
             owner = dp_device(k)
             remote(raw_part.at[ranks(owner)], raw_slots.at[d], dp_send, dp_recv, (owner, t)).start()
         raw_slots[d] = raw_part[ranks(d)]
@@ -247,7 +248,7 @@
 
         remote(raw_slots.at[0:7], raw_slots.at[0:7], dp_send, dp_recv, sibling).wait_recv()
         raw[ranks(d)] = jnp.sum(raw_slots[...], axis=0)
-        for k in (6, 2, 5, 7, 1, 3, 4):
+        for k in DP_OFFSETS:
             remote(raw.at[ranks(d)], raw.at[ranks(d)], dpg_send, dpg_recv, (dp_device(k), t)).start()
 
         @pl.when(step < ITERS)
@@ -295,7 +296,7 @@
 
 def shards(gradient, error_in, warm_start):
     dma = pltpu.SemaphoreType.DMA
-    block = pl.BlockSpec((1, BLOCK, COLS), lambda i: (0, i, 0))
+    block = pl.BlockSpec((1, 1024, COLS), lambda i: (0, i, 0))
     whole = pl.BlockSpec(memory_space=pltpu.VMEM)
     basis_terms, right = pl.pallas_call(
         kernel,
@@ -345,12 +346,12 @@
     return pl.pallas_call(
         finish,
         name="error_feedback",
-        grid=(D // BLOCK,),
+        grid=(D // 1024,),
         out_shape=(
             jax.ShapeDtypeStruct((R, COLS), F32),
             jax.ShapeDtypeStruct((1, D, COLS), BF16),
         ),
-        in_specs=[block, block, pl.BlockSpec((BLOCK, 4 * R), lambda i: (i, 0)), whole],
+        in_specs=[block, block, pl.BlockSpec((1024, 4 * R), lambda i: (i, 0)), whole],
         out_specs=(whole, block),
         compiler_params=pltpu.CompilerParams(vmem_limit_bytes=VMEM_LIMIT),
     )(gradient, error_in, basis_terms, right)

time: 168 us -> 157 us (0.935)
  Pallas kernels: 168 us -> 156 us
    pallas_call x1, Pallas kernels: 156 us -> 146 us  [shards(): pl.pallas_call(kernel, name='power_iterations', out_shape=(jax.ShapeDtype...]
    pallas_call x1, Pallas kernels: 11.9 us -> 9.25 us  [shards(): pl.pallas_call(finish, name='error_feedback', grid=(D // 1024,), out_shap...]
where the time goes in v3:
time: 157 us
  Pallas kernels  156 us (99%)
    pallas_call x1, Pallas kernels, shards(): pl.pallas_call(kernel, name='power_iterations', out_shape=(jax.ShapeDtype...  146 us
    pallas_call x1, Pallas kernels, shards(): pl.pallas_call(finish, name='error_feedback', grid=(D // 1024,), out_shap...  9.25 us

profile of v3, /device:TPU:1, one launch (start us, length us, event | category | flops | bytes accessed | tf_op | source)
XLA Modules:
  0.0 157.3 jit_solution(12920730421960134903)
XLA Ops:
  0.6 0.0 copy-start
  0.6 0.9 copy-done
  1.6 146.4 %power_iterations.1 = (bf16[4096,256]{1,0:T(8,128)(2,1)S(1)}, f32[64,896]{1,0:T(8,128)S(1)}) custom-call(bf16[1,4096,896]{2,1,0:T(8,128)(2,1)} %gradient.3, bf16[1,4096,896]{2,1,0:T(8,128)(2,1)} %error.3, f32[64,896]{1,0:T(8,128)S(1)} %copy-done), custom_call_target="tpu_custom_call" | custom-call | tf_op jit(solution)/shard_map/power_iterations/pallas_call | solution.py:301
  148.0 9.3 %error_feedback.1 = (f32[64,896]{1,0:T(8,128)}, bf16[1,4096,896]{2,1,0:T(8,128)(2,1)}) custom-call(bf16[1,4096,896]{2,1,0:T(8,128)(2,1)} %gradient.3, bf16[1,4096,896]{2,1,0:T(8,128)(2,1)} %error.3, bf16[4096,256]{1,0:T(8,128)(2,1)S(1)} %get-tuple-element.4.basis_terms, f32[64,896]{1,0:T(8,128)S(1)} %get-tuple-element.5.right), custom_call_target="tpu_custom_call" | custom-call | tf_op jit(solution)/shard_map/error_feedback/pallas_call | solution.py:346
Async XLA Ops:
  0.6 0.9 copy-start

commit v4 on v3

--- a/solution.py
+++ b/solution.py
@@ -13,7 +13,7 @@
 CHUNKS = 4
 ROWS = D // CHUNKS
 PIECE = 16
-BLOCK = 512
+BLOCK = 1024
 VMEM_LIMIT = 46 * 1024 * 1024
 MESH = pl.DeviceIdType.MESH
 F32 = jnp.float32
@@ -75,8 +75,8 @@
 
 
 def kernel(
-    gradient, error, warm, basis_terms, right_out,
-    both, turned, rr, part, cross, mine, slots, left, flat, raw_part, raw_slots, raw, sweeps,
+    gradient, error, warm, flat, second_out, right_out,
+    both, turned, rr, part, cross, mine, slots, left, raw_part, raw_slots, raw, first_sweep,
     load_sem, cross_send, cross_recv, rs_send, rs_recv, ag_send, ag_recv, fwd_send, fwd_recv,
     dp_send, dp_recv, dpg_send, dpg_recv,
 ):
@@ -88,11 +88,16 @@
     chip = place * 4 + z
     own = group * 32 + c * 16 + place
 
-    def device(i, j, k):
-        return ((j % 2) * 4 + i, (j // 2) * 8 + k * 2 + c)
+    xs = [(x + i) % 4 for i in range(4)]
+    ys = [(y + i) % 4 for i in range(4)]
+    dp_of_y = [(j % 2) * 4 for j in ys]
+    tensor_of_y = [(j // 2) * 8 for j in ys]
+    tensor_of_z = [((z + i) % 4) * 2 + c for i in range(4)]
+    xs_places = [i * 4 for i in xs]
+    dp_of_step = [((d // 4 + i) % 2) * 4 for i in range(2)]
 
     def away(o):
-        return device((x + o[0]) % 4, (y + o[1]) % 4, (z + o[2]) % 4)
+        return (dp_of_y[o[1]] + xs[o[0]], tensor_of_y[o[1]] + tensor_of_z[o[2]])
 
     sibling = (d, (t // 2) * 2 + other)
 
@@ -149,20 +154,18 @@
     def scatter_chunk(j):
         cross_copy(j).wait_recv()
         mine[j] = part[pl.ds(j * 32 + c * 16, 16)] + cross[j]
-        for r in (10, 2, 8, 6, 14, 9, 11, 5, 7, 13, 15, 1, 3, 4, 12, 0):
-            i, k = (x + r // 4) % 4, (y + r % 4) % 4
-            copy = remote(mine.at[j, i * 4 + k], slots.at[chip], rs_send, rs_recv, device(i, k, (j - i - k + 8) % 4))
-            if r:
-                copy.start()
-            else:
-
-                @pl.when(j != group)
-                def _():
-                    copy.start()
-
-                @pl.when(j == group)
-                def _():
+        def send_from(g):
+            @pl.when(group == g)
+            def _():
+                for o in OFFSETS:
+                    if (sum(o) + g - j) % 4 == 0:
+                        source = mine.at[j, xs_places[o[0]] + ys[o[1]]]
+                        remote(source, slots.at[chip], rs_send, rs_recv, away(o)).start()
+                if g == j:
                     slots[chip] = mine[j, place]
+
+        for g in range(4):
+            send_from(g)
 
     def gathered(j):
         @pl.when(j == group)
@@ -191,7 +194,7 @@
         return carry
 
     def dp_device(o):
-        return ((d // 4 + o[0]) % 2) * 4 + (x + o[1]) % 4
+        return dp_of_step[o[0]] + xs[o[1]]
 
     def ranks(owner):
         return pl.ds(pl.multiple_of(owner * 8, 8), 8)
@@ -210,7 +213,6 @@
                 keep(j, jnp.dot(rr[...], turned[:, row_chunk(j)], preferred_element_type=F32))
 
             cross_copy(j).start()
-
             return carry
 
         lax.fori_loop(0, CHUNKS, left_step, 0)
@@ -222,11 +224,11 @@
         @pl.when(step == 0)
         def _():
             def turn(j, carry):
-                rows = pl.ds(pl.multiple_of(j * BLOCK, BLOCK), BLOCK)
+                rows = row_chunk(j)
                 turned[:, rows] = both[rows, :].T
                 return carry
 
-            lax.fori_loop(0, D // BLOCK, turn, 0)
+            lax.fori_loop(0, CHUNKS, turn, 0)
 
         raw_part[...] = jnp.zeros_like(raw_part)
         remote(slots.at[0:63], slots.at[0:63], rs_send, rs_recv, sibling).wait_recv()
@@ -244,7 +246,7 @@
 
         @pl.when(step < ITERS)
         def _():
-            sweeps[0] = inverse_cholesky(contract(flat[...], flat[...], 1, 1, HIGHEST))
+            first_sweep[...] = inverse_cholesky(contract(flat[...], flat[...], 1, 1, HIGHEST))
 
         remote(raw_slots.at[0:7], raw_slots.at[0:7], dp_send, dp_recv, sibling).wait_recv()
         raw[ranks(d)] = jnp.sum(raw_slots[...], axis=0)
@@ -253,18 +255,12 @@
 
         @pl.when(step < ITERS)
         def _():
-            first = sweeps[0]
+            first = first_sweep[...]
             left_one = jnp.dot(first, flat[...], precision=HIGHEST, preferred_element_type=F32)
             flat[...] = left_one
             second = inverse_cholesky(contract(left_one, left_one, 1, 1, HIGHEST))
-            sweeps[1] = second
-            sweeps[0] = jnp.dot(second, first, precision=HIGHEST, preferred_element_type=F32) * (1.0 / REPL)
-
-        @pl.when(step == ITERS - 1)
-        def _():
-            basis = jnp.dot(sweeps[1], flat[...], precision=HIGHEST, preferred_element_type=F32)
-            high, middle, _ = terms(basis)
-            basis_terms[...] = jnp.concatenate([high, middle, high, middle], axis=0).T
+            second_out[...] = second
+            first_sweep[...] = jnp.dot(second, first, precision=HIGHEST, preferred_element_type=F32) * (1.0 / REPL)
 
         for j in range(CHUNKS):
             cross_copy(j).wait_send()
@@ -274,7 +270,7 @@
         remote(raw_slots.at[0:7], raw_slots.at[0:7], dp_send, dp_recv, sibling).wait_send()
         remote(raw_slots.at[0:7], raw_slots.at[0:7], dpg_send, dpg_recv, sibling).wait()
 
-        right = jnp.dot(sweeps[0], raw[...], precision=HIGHEST, preferred_element_type=F32)
+        right = jnp.dot(first_sweep[...], raw[...], precision=HIGHEST, preferred_element_type=F32)
         right_out[...] = right
         set_right(right)
         return 0
@@ -282,27 +278,32 @@
     lax.fori_loop(0, ITERS, iteration, 0)
 
 
-def finish(gradient, error, basis_terms, right, right_out, error_out):
+def finish(gradient, error, left_one, second, right, right_out, error_out):
     @pl.when(pl.program_id(0) == 0)
     def _():
         right_out[...] = right[...]
 
     high, middle, _ = terms(right[...])
     right_terms = jnp.concatenate([high, high, middle, middle], axis=0)
-    approx = jnp.dot(basis_terms[...], right_terms, preferred_element_type=F32)
+    rows = pl.ds(pl.multiple_of(pl.program_id(0) * BLOCK, BLOCK), BLOCK)
+    basis = jnp.dot(second[...], left_one[:, rows], precision=HIGHEST, preferred_element_type=F32)
+    basis_high, basis_middle, _ = terms(basis)
+    basis_terms = jnp.concatenate([basis_high, basis_middle, basis_high, basis_middle], axis=0).T
+    approx = jnp.dot(basis_terms, right_terms, preferred_element_type=F32)
     merged = gradient[0].astype(F32) + error[0].astype(F32)
     error_out[0] = (merged - approx).astype(BF16)
 
 
 def shards(gradient, error_in, warm_start):
     dma = pltpu.SemaphoreType.DMA
-    block = pl.BlockSpec((1, 1024, COLS), lambda i: (0, i, 0))
+    block = pl.BlockSpec((1, BLOCK, COLS), lambda i: (0, i, 0))
     whole = pl.BlockSpec(memory_space=pltpu.VMEM)
-    basis_terms, right = pl.pallas_call(
+    left_one, second, right = pl.pallas_call(
         kernel,
         name="power_iterations",
         out_shape=(
-            jax.ShapeDtypeStruct((D, 4 * R), BF16),
+            jax.ShapeDtypeStruct((R, D), F32),
+            jax.ShapeDtypeStruct((R, R), F32),
             jax.ShapeDtypeStruct((R, COLS), F32),
         ),
         in_specs=[
@@ -310,7 +311,7 @@
             pl.BlockSpec(memory_space=pltpu.HBM),
             whole,
         ],
-        out_specs=(whole, whole),
+        out_specs=(whole, whole, whole),
         scratch_shapes=[
             pltpu.VMEM((D, 2 * COLS), BF16),
             pltpu.VMEM((2 * COLS, D), BF16),
@@ -320,11 +321,10 @@
             pltpu.VMEM((CHUNKS, 16, PIECE, 128), F32),
             pltpu.VMEM((64, PIECE, 128), F32),
             pltpu.VMEM((128, PIECE, 128), F32),
-            pltpu.VMEM((R, D), F32),
             pltpu.VMEM((R, COLS), F32),
             pltpu.VMEM((REPL, 8, COLS), F32),
             pltpu.VMEM((R, COLS), F32),
-            pltpu.VMEM((2, R, R), F32),
+            pltpu.VMEM((R, R), F32),
             dma((CHUNKS, 2)),
             dma((CHUNKS,)),
             dma((CHUNKS,)),
@@ -346,15 +346,15 @@
     return pl.pallas_call(
         finish,
         name="error_feedback",
-        grid=(D // 1024,),
+        grid=(D // BLOCK,),
         out_shape=(
             jax.ShapeDtypeStruct((R, COLS), F32),
             jax.ShapeDtypeStruct((1, D, COLS), BF16),
         ),
-        in_specs=[block, block, pl.BlockSpec((1024, 4 * R), lambda i: (i, 0)), whole],
+        in_specs=[block, block, whole, whole, whole],
         out_specs=(whole, block),
         compiler_params=pltpu.CompilerParams(vmem_limit_bytes=VMEM_LIMIT),
-    )(gradient, error_in, basis_terms, right)
+    )(gradient, error_in, left_one, second, right)
 
 
 def solution(mesh):

time: 157 us -> 155 us (0.987)
  Pallas kernels: 156 us -> 153 us
    pallas_call x1, Pallas kernels: 146 us -> 143 us  [shards(): pl.pallas_call(kernel, name='power_iterations', out_shape=(jax.ShapeDtype...]
where the time goes in v4:
time: 155 us
  Pallas kernels  153 us (99%)
    pallas_call x1, Pallas kernels, shards(): pl.pallas_call(kernel, name='power_iterations', out_shape=(jax.ShapeDtype...  143 us
    pallas_call x1, Pallas kernels, shards(): pl.pallas_call(finish, name='error_feedback', grid=(D // BLOCK,), out_sha...  9.81 us

profile of v4, /device:TPU:1, one launch (start us, length us, event | category | flops | bytes accessed | tf_op | source)
XLA Modules:
  0.0 154.6 jit_solution(13900545929786879686)
XLA Ops:
  0.6 0.0 copy-start
  0.6 0.9 copy-done
  1.6 143.2 %power_iterations.1 = (f32[64,4096]{1,0:T(8,128)S(1)}, f32[64,64]{1,0:T(8,128)S(1)}, f32[64,896]{1,0:T(8,128)S(1)}) custom-call(bf16[1,4096,896]{2,1,0:T(8,128)(2,1)} %gradient.3, bf16[1,4096,896]{2,1,0:T(8,128)(2,1)} %error.3, f32[64,896]{1,0:T(8,128)S(1)} %copy-done), custom_call_target="tpu_custom_call" | custom-call | tf_op jit(solution)/shard_map/power_iterations/pallas_call | solution.py:301
  144.8 9.8 %error_feedback.1 = (f32[64,896]{1,0:T(8,128)}, bf16[1,4096,896]{2,1,0:T(8,128)(2,1)}) custom-call(bf16[1,4096,896]{2,1,0:T(8,128)(2,1)} %gradient.3, bf16[1,4096,896]{2,1,0:T(8,128)(2,1)} %error.3, f32[64,4096]{1,0:T(8,128)S(1)} %get-tuple-element.5.left_one, f32[64,64]{1,0:T(8,128)S(1)} %get-tuple-element.6.second, f32[64,896]{1,0:T(8,128)S(1)} %get-tuple-element.7.right), custom_call_target="tpu_custom_call" | custom-call | tf_op jit(solution)/shard_map/error_feedback/pallas_call | solution.py:346
Async XLA Ops:
  0.6 0.9 copy-start

commit v5 on v4

--- a/solution.py
+++ b/solution.py
@@ -215,11 +215,11 @@
             cross_copy(j).start()
             return carry
 
-        lax.fori_loop(0, CHUNKS, left_step, 0)
-        scatter_chunk(CHUNKS - 4)
-        scatter_chunk(CHUNKS - 3)
-        scatter_chunk(CHUNKS - 2)
-        scatter_chunk(CHUNKS - 1)
+        lax.fori_loop(0, CHUNKS - 1, left_step, 0)
+        scatter_chunk(0)
+        lax.fori_loop(CHUNKS - 1, CHUNKS, left_step, 0)
+        for j in range(1, CHUNKS):
+            scatter_chunk(j)
 
         @pl.when(step == 0)
         def _():

time: 155 us -> 157 us (1.013)
  Pallas kernels: 153 us -> 156 us
    pallas_call x1, Pallas kernels: 143 us -> 146 us  [shards(): pl.pallas_call(kernel, name='power_iterations', out_shape=(jax.ShapeDtype...]
where the time goes in v5:
time: 157 us
  Pallas kernels  156 us (99%)
    pallas_call x1, Pallas kernels, shards(): pl.pallas_call(kernel, name='power_iterations', out_shape=(jax.ShapeDtype...  146 us
    pallas_call x1, Pallas kernels, shards(): pl.pallas_call(finish, name='error_feedback', grid=(D // BLOCK,), out_sha...  9.84 us

profile of v5, /device:TPU:1, one launch (start us, length us, event | category | flops | bytes accessed | tf_op | source)
XLA Modules:
  0.0 157.2 jit_solution(11195010399457948699)
XLA Ops:
  0.6 0.0 copy-start
  0.6 0.9 copy-done
  1.6 145.8 %power_iterations.1 = (f32[64,4096]{1,0:T(8,128)S(1)}, f32[64,64]{1,0:T(8,128)S(1)}, f32[64,896]{1,0:T(8,128)S(1)}) custom-call(bf16[1,4096,896]{2,1,0:T(8,128)(2,1)} %gradient.3, bf16[1,4096,896]{2,1,0:T(8,128)(2,1)} %error.3, f32[64,896]{1,0:T(8,128)S(1)} %copy-done), custom_call_target="tpu_custom_call" | custom-call | tf_op jit(solution)/shard_map/power_iterations/pallas_call | solution.py:301
  147.4 9.8 %error_feedback.1 = (f32[64,896]{1,0:T(8,128)}, bf16[1,4096,896]{2,1,0:T(8,128)(2,1)}) custom-call(bf16[1,4096,896]{2,1,0:T(8,128)(2,1)} %gradient.3, bf16[1,4096,896]{2,1,0:T(8,128)(2,1)} %error.3, f32[64,4096]{1,0:T(8,128)S(1)} %get-tuple-element.5.left_one, f32[64,64]{1,0:T(8,128)S(1)} %get-tuple-element.6.second, f32[64,896]{1,0:T(8,128)S(1)} %get-tuple-element.7.right), custom_call_target="tpu_custom_call" | custom-call | tf_op jit(solution)/shard_map/error_feedback/pallas_call | solution.py:346
Async XLA Ops:
  0.6 0.9 copy-start
